TPU v7x, 32 devices: a whole 2x2x4 slice. The times are simulated.
32 devices in a mesh: groups: 2 (over x), ctx: 16 (over z, y, core).
Axes of the slice: x: 2, y: 2, z: 4, core: 2. Of those that a mesh axis runs over, the one named last changes fastest.
Arguments:
- raster_tokens: bfloat16 [4096, 1024], P(('groups', 'ctx')), parts along dimension 0, may hold values from -45 to 45
- hilbert_perm: int32 [4096], P(('groups', 'ctx')), parts along dimension 0, may hold values from 0 to 2047, as said below
- neighbors: int32 [32, 5], P(('groups', 'ctx')), parts along dimension 0, may hold values from 0 to 15, as said below
- neighbor_counts: int32 [32], P(('groups', 'ctx')), parts along dimension 0, may hold values from 1 to 5, as said below
- norm_gain: float32 [1024], replicated, may hold values from 0.1 to 1.9
- w_qkv: bfloat16 [1024, 3072], replicated, may hold values from -0.8125 to 0.8125
- w_out: bfloat16 [1024, 1024], replicated, may hold values from -0.5 to 0.5
- cotangent: bfloat16 [4096, 1024], P(('groups', 'ctx')), parts along dimension 0, may hold values from -6 to 6
Outputs:
- layer_out: bfloat16 [4096, 1024], P(('groups', 'ctx')), parts along dimension 0
- grad_tokens: bfloat16 [4096, 1024], P(('groups', 'ctx')), parts along dimension 0
- grad_w_out: float32 [2048, 1024], P(('groups', 'ctx')), parts along dimension 0
- grad_gain: float32 [2048], P('groups'), parts along dimension 0
There are 2 independent parts, one for each index of `groups`. A program takes and returns all parts, laid end to end along the dimension named above; an argument that names none is the same for every part. Nothing has to cross between parts.
Inputs may be any that keep to these rules, and one draw needn't show every extreme that they name: `hilbert_perm`: A permutation. Every 128 consecutive positions of the Hilbert order take exactly 8 tokens from every 128 consecutive raster tokens. `neighbors`: row b starts with b, followed by distinct blocks other than b at a distance of at most 4; entries from slot neighbor_counts[b] on equal b. `neighbor_counts`: the block itself is counted.
All inputs are finite; a program needn't handle non-finite values.
Results may differ from a plain program's by a relative error of at most 0.02.
The roundings to bfloat16 on the way count: a program that leaves them out, or rounds other values in their place, can miss the bound.
Values may be sent and summed in bfloat16 or wider, within the bound.
A program may use at most 128 MiB of HBM per device.

v0:
```python
import jax
import jax.numpy as jnp
from jax import lax
from jax.sharding import PartitionSpec as P

HEADS = 16
BLOCK = 128
REACH = 4


EPS = 1e-06
FAR = -1e30


def from_behind(block, axis, distance):
    devices = range(lax.axis_size(axis))
    route = [(i - distance, i) for i in devices if i - distance in devices]
    return lax.ppermute(block, axis, route)


def softmax_probs(heads_q, heads_k, counts, score_scale):
    scores = (
        jnp.einsum("sqhd,skhd->shqk", heads_q, heads_k, preferred_element_type=jnp.float32)
        * score_scale
    )
    slot_of = jnp.arange(heads_k.shape[1]) // BLOCK
    usable = slot_of[None, :] < counts[:, None]
    scores = jnp.where(usable[:, None, None, :], scores, FAR)
    row_max = jnp.max(scores, axis=-1, keepdims=True)
    shifted = jnp.exp(scores - row_max)
    return shifted / jnp.sum(shifted, axis=-1, keepdims=True)


def per_device(
    raster_tokens, hilbert_perm, neighbors, neighbor_counts, norm_gain, w_qkv, w_out, cotangent
):
    axis_size = lax.axis_size("ctx")
    my_index = lax.axis_index("ctx")
    tok_rows, model_width = raster_tokens.shape
    per_peer = tok_rows // axis_size
    per_dev = tok_rows // BLOCK
    reach_dev = (REACH + per_dev - 1) // per_dev
    head_dim = model_width // HEADS
    score_scale = head_dim ** (-0.5)
    norm_scale = (tok_rows * axis_size) ** (-0.5)
    source_dev = hilbert_perm // tok_rows
    local_row = hilbert_perm % tok_rows
    sorted_rows = jnp.argsort(source_dev, stable=True)
    wanted = local_row[sorted_rows].reshape(axis_size, per_peer)
    requested = lax.all_to_all(wanted, "ctx", split_axis=0, concat_axis=0, tiled=True)
    requested_flat = requested.reshape(-1)
    outgoing = raster_tokens[requested_flat].reshape(axis_size, per_peer, model_width)
    arrived = lax.all_to_all(outgoing, "ctx", split_axis=0, concat_axis=0, tiled=True)
    ordered = (
        jnp.zeros_like(raster_tokens).at[sorted_rows].set(arrived.reshape(tok_rows, model_width))
    )
    ordered_f = ordered.astype(jnp.float32)
    inv_rms = lax.rsqrt(jnp.mean(ordered_f * ordered_f, axis=-1, keepdims=True) + EPS)
    normed = (ordered_f * inv_rms * norm_gain).astype(jnp.bfloat16)
    projected = jnp.dot(normed, w_qkv, preferred_element_type=jnp.float32).astype(jnp.bfloat16)
    queries = projected[:, :model_width]
    keys_vals = projected[:, model_width:]
    kv_weight = w_qkv[:, model_width:]
    from_lower = []
    from_upper = []
    carry_low = normed
    carry_high = normed
    for distance in range(reach_dev):
        carry_low = from_behind(carry_low, "ctx", 1)
        carry_high = from_behind(carry_high, "ctx", -1)
        from_lower.append(carry_low)
        from_upper.append(carry_high)
    remote_low = [
        jnp.dot(remote_piece, kv_weight, preferred_element_type=jnp.float32).astype(jnp.bfloat16)
        for remote_piece in from_lower
    ]
    remote_high = [
        jnp.dot(remote_piece, kv_weight, preferred_element_type=jnp.float32).astype(jnp.bfloat16)
        for remote_piece in from_upper
    ]
    window = jnp.concatenate(remote_low[::-1] + [keys_vals] + remote_high, axis=0)
    window_blocks = window.reshape(-1, BLOCK, 2 * model_width)
    slot_index = neighbors - (my_index - reach_dev) * per_dev
    gathered = window_blocks[slot_index].reshape(per_dev, -1, 2 * model_width)
    heads_k = gathered[:, :, :model_width].reshape(per_dev, -1, HEADS, head_dim)
    heads_v = gathered[:, :, model_width:].reshape(per_dev, -1, HEADS, head_dim)
    heads_q = queries.reshape(per_dev, BLOCK, HEADS, head_dim)
    weights_f = softmax_probs(heads_q, heads_k, neighbor_counts, score_scale)
    probs_b = weights_f.astype(jnp.bfloat16)
    attended = jnp.einsum("shqk,skhd->sqhd", probs_b, heads_v, preferred_element_type=jnp.float32)
    attended = attended.reshape(tok_rows, model_width).astype(jnp.bfloat16)
    projected_out = jnp.dot(attended, w_out, preferred_element_type=jnp.float32)
    layer_out = (ordered_f + projected_out).astype(jnp.bfloat16)
    grad_w_out = None
    d_attended = jnp.dot(cotangent, w_out.T, preferred_element_type=jnp.float32).astype(
        jnp.bfloat16
    )
    d_heads = d_attended.reshape(per_dev, BLOCK, HEADS, head_dim)
    d_probs = jnp.einsum("sqhd,skhd->shqk", d_heads, heads_v, preferred_element_type=jnp.float32)
    row_dots = jnp.sum(d_probs * weights_f, axis=-1, keepdims=True)
    d_scores = (weights_f * (d_probs - row_dots) * score_scale).astype(jnp.bfloat16)
    d_query = jnp.einsum("shqk,skhd->sqhd", d_scores, heads_k, preferred_element_type=jnp.float32)
    d_query = d_query.reshape(tok_rows, model_width).astype(jnp.bfloat16)
    d_keys = jnp.einsum("shqk,sqhd->skhd", d_scores, heads_q, preferred_element_type=jnp.float32)
    d_vals = jnp.einsum("shqk,sqhd->skhd", probs_b, d_heads, preferred_element_type=jnp.float32)
    contrib = jnp.concatenate(
        [d_keys.reshape(-1, BLOCK, model_width), d_vals.reshape(-1, BLOCK, model_width)], axis=-1
    )
    summed = jnp.zeros(window_blocks.shape, jnp.float32).at[slot_index.reshape(-1)].add(contrib)
    partials = summed.astype(jnp.bfloat16)
    accum = partials[reach_dev].astype(jnp.float32)
    for distance in range(1, reach_dev + 1):
        accum = accum + from_behind(partials[reach_dev + distance], "ctx", distance).astype(
            jnp.float32
        )
        accum = accum + from_behind(partials[reach_dev - distance], "ctx", -distance).astype(
            jnp.float32
        )
    d_kv = accum.astype(jnp.bfloat16)
    d_proj = jnp.concatenate([d_query, d_kv], axis=-1)
    d_normed = jnp.dot(d_proj, w_qkv.T, preferred_element_type=jnp.float32)
    gain_term = jnp.sum(d_normed * ordered_f * inv_rms, axis=0)
    grad_gain = lax.psum(gain_term, "ctx") * norm_scale
    scaled = d_normed * norm_gain
    d_ordered = (
        cotangent.astype(jnp.float32)
        + inv_rms * scaled
        - ordered_f * inv_rms**3 * jnp.mean(scaled * ordered_f, axis=-1, keepdims=True)
    )
    d_ordered = d_ordered.astype(jnp.bfloat16)
    leaving = d_ordered[sorted_rows].reshape(axis_size, per_peer, model_width)
    returned = lax.all_to_all(leaving, "ctx", split_axis=0, concat_axis=0, tiled=True)
    grad_tokens = (
        jnp.zeros_like(raster_tokens)
        .at[requested_flat]
        .set(returned.reshape(tok_rows, model_width))
    )
    grad_w_out = (
        lax.psum_scatter(
            lax.dot_general(
                attended, cotangent, (((0,), (0,)), ((), ())), preferred_element_type=jnp.float32
            ),
            "ctx",
            scatter_dimension=0,
            tiled=True,
        )
        * norm_scale
    )
    return (layer_out, grad_tokens, grad_w_out, grad_gain)


def solution(mesh):
    placed = (
        P(("groups", "ctx"), None),
        P(("groups", "ctx")),
        P(("groups", "ctx"), None),
        P(("groups", "ctx")),
        P(),
        P(),
        P(),
        P(("groups", "ctx"), None),
    )
    return jax.shard_map(
        per_device,
        mesh=mesh,
        in_specs=placed,
        out_specs=(
            P(("groups", "ctx"), None),
            P(("groups", "ctx"), None),
            P(("groups", "ctx"), None),
            P("groups"),
        ),
        check_vma=False,
    )
```

profile of v0, /device:TPU:0, one launch (start us, length us, event | category | flops | bytes accessed | tf_op | source)
XLA Modules:
  0.0 316.1 jit_solution(17017370256104363028)
XLA Ops:
  11.9 13.6 %all_to_all.19 = s32[16,1,8]{2,1,0:T(1,128)S(1)} all-to-all(s32[16,1,8]{2,1,0:T(1,128)S(1)} %bitcast.117), channel_id=1, replica_groups=mesh['groups'=2,'ctx'=16] {'ctx'}, dimensions={0} | all-to-all | bytes 1024 | tf_op jit(solution)/shard_map/all_to_all | solution.py:50
  28.8 12.6 %all_to_all.20 = bf16[16,8,1024]{2,1,0:T(8,128)(2,1)S(1)} all-to-all(bf16[16,8,1024]{2,1,0:T(8,128)(2,1)S(1)} %bitcast.109), channel_id=1, replica_groups=mesh['groups'=2,'ctx'=16] {'ctx'}, dimensions={0} | all-to-all | bytes 524288 | tf_op jit(solution)/shard_map/all_to_all | solution.py:53
  46.7 4.6 %collective-permute-start.1 = (bf16[128,1024]{1,0:T(8,128)(2,1)S(1)}, bf16[128,1024]{1,0:T(8,128)(2,1)}, u32[]{:S(2)}, u32[]{:S(2)}) collective-permute-start(bf16[128,1024]{1,0:T(8,128)(2,1)S(1)} %collective-permute-done), channel_id=1, source_target_pairs={{0,1},{1,2},{2,3},{3,4},{4,5},{5,6},{6,7},{7,8},{8,9},{9,10},{10,1... | collective-permute-start | bytes 786440 | tf_op jit(solution)/shard_map/ppermute | solution.py:18
  52.6 6.4 %collective-permute-start.2 = (bf16[128,1024]{1,0:T(8,128)(2,1)}, bf16[128,1024]{1,0:T(8,128)(2,1)}, u32[]{:S(2)}, u32[]{:S(2)}) collective-permute-start(bf16[128,1024]{1,0:T(8,128)(2,1)} %collective-permute-done.1), channel_id=1, source_target_pairs={{0,1},{1,2},{2,3},{3,4},{4,5},{5,6},{6,7},{7,8},{8,9},{9,10},{10,1... | collective-permute-start | bytes 786440 | tf_op jit(solution)/shard_map/ppermute | solution.py:18
  61.0 6.4 %collective-permute-start.3 = (bf16[128,1024]{1,0:T(8,128)(2,1)}, bf16[128,1024]{1,0:T(8,128)(2,1)}, u32[]{:S(2)}, u32[]{:S(2)}) collective-permute-start(bf16[128,1024]{1,0:T(8,128)(2,1)} %collective-permute-done.2), channel_id=1, source_target_pairs={{0,1},{1,2},{2,3},{3,4},{4,5},{5,6},{6,7},{7,8},{8,9},{9,10},{10,1... | collective-permute-start | bytes 786440 | tf_op jit(solution)/shard_map/ppermute | solution.py:18
  67.4 3.8 %convolution_convert_fusion = bf16[128,3072]{1,0:T(8,128)(2,1)S(1)} fusion(bf16[128,1024]{1,0:T(8,128)(2,1)S(1)} %fusion.60, bf16[1024,3072]{1,0:T(8,128)(2,1)} %param.13), kind=kOutput, calls=%fused_computation.16 | convolution fusion | flops 805699584 | bytes 7340032 | tf_op jit(solution)/shard_map/dot_general | solution.py:60
  73.4 3.1 fusion.24
  76.6 3.1 fusion.23
  90.7 4.7 %gather_fusion.2 = bf16[5,128,2048]{2,1,0:T(8,128)(2,1)} fusion(bf16[9,128,2048]{2,1,0:T(8,128)(2,1)} %bitcast.106, s32[1024]{0:T(1024)S(1)} %pad_clamp_fusion), kind=kCustom, calls=%fused_computation.2 | custom fusion | bytes 5242900 | tf_op jit(solution)/shard_map/gather | solution.py:84
  95.5 3.5 %fusion.89 = (bf16[1,640,1024]{2,1,0:T(8,128)(2,1)}, bf16[1,640,1024]{2,1,0:T(8,128)(2,1)}) fusion(bf16[1,640,2048]{2,1,0:T(8,128)(2,1)} %bitcast.103), kind=kLoop, calls=%fused_computation.138 | loop fusion | bytes 5242880 | tf_op jit(solution)/shard_map/slice | solution.py:85
  103.9 5.5 %fusion.90 = (f32[16,128]{1,0:T(8,128)S(1)}, f32[16,128,640]{2,1,0:T(8,128)}) fusion(pred[640]{0:T(1024)(128)(4,1)S(1)} %fusion.75, bf16[128,16,64]{0,2,1:T(8,128)(2,1)S(1)} %bitcast.114, bf16[640,16,64]{0,2,1:T(8,128)(2,1)} %bitcast.107), kind=kOutput, calls=%fused_computation.139 | convolution fusion | flops 173015680 | bytes 6824576 | tf_op jit(solution)/shard_map/sub | solution.py:30
  109.4 4.1 %fusion.31 = bf16[16,64,128]{2,1,0:T(8,128)(2,1)S(1)} fusion(bf16[640,16,64]{0,2,1:T(8,128)(2,1)} %bitcast.104, f32[16,128,640]{2,1,0:T(8,128)} %get-tuple-element.23, f32[16,128]{1,0:T(8,128)S(1)} %get-tuple-element.22), kind=kOutput, calls=%fused_computation.47 | convolution fusion | flops 170524672 | bytes 6823936 | tf_op jit(solution)/shard_map/shqk,skhd->sqhd/dot_general | solution.py:90
  117.3 4.6 %convolution_bitcast_fusion = f32[1,640,16,64]{1,3,2,0:T(8,128)} fusion(bf16[128,16,64]{0,2,1:T(8,128)(2,1)S(1)} %bitcast.112, f32[16,128,640]{2,1,0:T(8,128)} %get-tuple-element.23, f32[16,128]{1,0:T(8,128)S(1)} %get-tuple-element.22), kind=kOutput, calls=%fused_computation.42 | convolution fusion | flops 170393600 | bytes 8134656 | tf_op jit(solution)/shard_map/shqk,sqhd->skhd/dot_general | solution.py:105
  121.9 4.4 %reshape.226 = f32[5,128,1024]{1,0,2:T(8,128)} reshape(f32[1,640,16,64]{1,3,2,0:T(8,128)} %convolution_bitcast_fusion) | data formatting | bytes 5242880 | tf_op jit(solution)/shard_map/reshape | solution.py:107
  126.3 4.7 %fusion.91 = f32[16,128,640]{2,1,0:T(8,128)} fusion(bf16[128,16,64]{0,2,1:T(8,128)(2,1)S(1)} %bitcast.113, bf16[640,16,64]{0,2,1:T(8,128)(2,1)} %bitcast.105), kind=kOutput, calls=%fused_computation.140 | convolution fusion | flops 167772160 | bytes 6815744 | tf_op jit(solution)/shard_map/sqhd,skhd->shqk/dot_general | solution.py:99
  131.0 19.2 %fusion.25 = f32[1,640,16,64]{1,3,2,0:T(8,128)} fusion(bf16[128,16,64]{0,2,1:T(8,128)(2,1)S(1)} %bitcast.115, f32[16,128,640]{2,1,0:T(8,128)} %fusion.91, f32[16,128,640]{2,1,0:T(8,128)} %get-tuple-element.23, f32[16,128]{1,0:T(8,128)S(1)} %get-tuple-element.22), kind=kOutput, calls=%fused_computation.41 | convolution fusion | flops 176949888 | bytes 13377536 | tf_op jit(solution)/shard_map/shqk,sqhd->skhd/dot_general | solution.py:104
  150.2 4.4 %reshape.225 = f32[5,128,1024]{1,0,2:T(8,128)} reshape(f32[1,640,16,64]{1,3,2,0:T(8,128)} %fusion.25) | data formatting | bytes 5242880 | tf_op jit(solution)/shard_map/reshape | solution.py:107
  154.7 6.8 %pad_maximum_fusion = f32[5,128,2048]{1,0,2:T(8,128)} fusion(f32[5,128,1024]{1,0,2:T(8,128)} %reshape.226, f32[5,128,1024]{1,0,2:T(8,128)} %reshape.225), kind=kLoop, calls=%fused_computation.9 | loop fusion | flops 1310720 | bytes 10485760 | tf_op jit(solution)/shard_map/concatenate | solution.py:106
  161.4 7.9 %copy.30 = f32[5,128,2048]{2,1,0:T(8,128)} copy(f32[5,128,2048]{1,0,2:T(8,128)} %pad_maximum_fusion) | data formatting | bytes 10485760 | tf_op jit(solution)/shard_map/concatenate | solution.py:106
  169.3 4.8 %broadcast_in_dim.22 = f32[9,128,2048]{2,1,0:T(8,128)} broadcast(f32[]{:T(128)} %constant.63.clone.1), dimensions={} | broadcast | bytes 9437188 | tf_op jit(solution)/shard_map/broadcast_in_dim | solution.py:109
  174.2 12.3 %scatter_fusion = f32[9,128,2048]{2,1,0:T(8,128)} fusion(f32[9,128,2048]{2,1,0:T(8,128)} %broadcast_in_dim.22, s32[5]{0:T(128)S(1)} %fusion.81, f32[5,128,2048]{2,1,0:T(8,128)} %copy.30), kind=kCustom, calls=%fused_computation.5 | custom fusion | flops 1310720 | bytes 15728660 | tf_op jit(solution)/shard_map/scatter-add | solution.py:109
  186.5 4.5 %convert_element_type.137 = bf16[9,128,2048]{2,1,0:T(8,128)(2,1)S(1)} convert(f32[9,128,2048]{2,1,0:T(8,128)} %scatter_fusion) | non-fusion elementwise | flops 2359296 | bytes 14155776 | tf_op jit(solution)/shard_map/convert_element_type | solution.py:110
  194.6 5.4 %collective-permute-start.8 = (bf16[128,2048]{1,0:T(8,128)(2,1)S(1)}, bf16[128,2048]{1,0:T(8,128)(2,1)}, u32[]{:S(2)}, u32[]{:S(2)}) collective-permute-start(bf16[128,2048]{1,0:T(8,128)(2,1)S(1)} %get-tuple-element.8), channel_id=1, source_target_pairs={{0,1},{1,2},{2,3},{3,4},{4,5},{5,6},{6,7},{7,8},{8,9},{9,10},{10,1... | collective-permute-start | bytes 1572872 | tf_op jit(solution)/shard_map/ppermute | solution.py:18
  201.3 7.2 %collective-permute-start.14 = (bf16[128,2048]{1,0:T(8,128)(2,1)S(1)}, bf16[128,2048]{1,0:T(8,128)(2,1)}, u32[]{:S(2)}, u32[]{:S(2)}) collective-permute-start(bf16[128,2048]{1,0:T(8,128)(2,1)S(1)} %get-tuple-element.10), channel_id=1, source_target_pairs={{0,4},{1,5},{2,6},{3,7},{4,8},{5,9},{6,10},{7,11},{8,12},{9,13},{1... | collective-permute-start | bytes 1572872 | tf_op jit(solution)/shard_map/ppermute | solution.py:18
  210.1 6.6 %collective-permute-start.12 = (bf16[128,2048]{1,0:T(8,128)(2,1)}, bf16[128,2048]{1,0:T(8,128)(2,1)}, u32[]{:S(2)}, u32[]{:S(2)}) collective-permute-start(bf16[128,2048]{1,0:T(8,128)(2,1)} %get-tuple-element.12), channel_id=1, source_target_pairs={{0,3},{1,4},{2,5},{3,6},{4,7},{5,8},{6,9},{7,10},{8,11},{9,12},{10... | collective-permute-start | bytes 1572872 | tf_op jit(solution)/shard_map/ppermute | solution.py:18
  218.7 4.6 %collective-permute-start.10 = (bf16[128,2048]{1,0:T(8,128)(2,1)}, bf16[128,2048]{1,0:T(8,128)(2,1)}, u32[]{:S(2)}, u32[]{:S(2)}) collective-permute-start(bf16[128,2048]{1,0:T(8,128)(2,1)} %get-tuple-element.14), channel_id=1, source_target_pairs={{0,2},{1,3},{2,4},{3,5},{4,6},{5,7},{6,8},{7,9},{8,10},{9,11},{10,... | collective-permute-start | bytes 1572872 | tf_op jit(solution)/shard_map/ppermute | solution.py:18
  224.6 19.1 %fusion.34 = bf16[16,64,128]{2,1,0:T(8,128)(2,1)S(1)} fusion(bf16[640,16,64]{0,2,1:T(8,128)(2,1)} %bitcast.108, f32[16,128,640]{2,1,0:T(8,128)} %fusion.91, f32[16,128,640]{2,1,0:T(8,128)} %get-tuple-element.23, f32[16,128]{1,0:T(8,128)S(1)} %get-tuple-element.22), kind=kOutput, calls=%fused_computation.48 | convolution fusion | flops 177080960 | bytes 12066816 | tf_op jit(solution)/shard_map/shqk,skhd->sqhd/dot_general | solution.py:102
  245.6 9.2 %collective-permute-done.10 = bf16[128,2048]{1,0:T(8,128)(2,1)} collective-permute-done((bf16[128,2048]{1,0:T(8,128)(2,1)}, bf16[128,2048]{1,0:T(8,128)(2,1)}, u32[]{:S(2)}, u32[]{:S(2)}) %collective-permute-start.10) | collective-permute-done | bytes 524320 | tf_op jit(solution)/shard_map/ppermute | solution.py:18
  254.9 3.1 fusion.45
  258.0 5.1 %fusion.66 = (f32[1024]{0:T(1024)S(1)}, f32[128]{0:T(128)S(1)}, f32[128,1024]{1,0:T(8,128)S(1)}) fusion(bf16[128,1024]{1,0:T(8,128)(2,1)S(1)} %scatter_custom_fusion, f32[128]{0:T(128)S(1)} %get-tuple-element.19, f32[1024]{0:T(1024)S(1)} %copy-done.6, bf16[1024,3072]{1,0:T(8,128)(2,1)} %param.13, bf16[128,2048]{1,0:T(8,128)(2,1)S(1)} %fusion.45, ...), kind=kOutput, calls=%fused_computation.85 | convolution fusion | flops 807795584 | bytes 7873536 | tf_op jit(solution)/shard_map/dot_general | solution.py:121
  264.9 5.2 %all-to-all-start.2 = ((bf16[16,8,1024]{2,1,0:T(8,128)(2,1)}), bf16[16,8,1024]{2,1,0:T(8,128)(2,1)S(1)}, u32[]{:S(2)}, u32[]{:S(2)}) async-start(bf16[16,8,1024]{2,1,0:T(8,128)(2,1)} %bitcast.33), calls=%async_computation.2 | async-start | bytes 524288 | tf_op jit(solution)/shard_map/all_to_all | solution.py:132
  271.3 33.8 %psum.7 = f32[1024]{0:T(1024)S(1)} all-reduce(f32[1024]{0:T(1024)S(1)} %get-tuple-element.6), channel_id=1, replica_groups=mesh['groups'=2,'ctx'=16] {'ctx'}, use_global_device_ids=true, to_apply=%region_11.12 | all-reduce | flops 1024 | bytes 8192 | tf_op jit(solution)/shard_map/psum | solution.py:123
  (101 shorter events, 56.2 us)
Async XLA Ops:
  7.2 109.1 %copy-start = (bf16[1024,1024]{1,0:T(8,128)(2,1)S(1)}, bf16[1024,1024]{1,0:T(8,128)(2,1)}, u32[]{:S(2)}) copy-start(bf16[1024,1024]{1,0:T(8,128)(2,1)} %param.14) | copy-start | bytes 6291460
  7.2 51.8 %copy-start.11 = (s32[1,5]{1,0:T(1,128)S(1)}, s32[1,5]{1,0:T(1,128)}, u32[]{:S(2)}) copy-start(s32[1,5]{1,0:T(1,128)} %param.10) | copy-start | bytes 64
  7.2 300.4 %reduce-scatter.2.cloned.1.call-start = ((), (), s32[]{:S(2)}) async-start(), calls=%async_computation.4 | async-start | bytes 4456448 | tf_op jit(solution)/shard_map/reduce_scatter | solution.py:139
  43.7 3.1 collective-permute-start
  45.4 5.9 %collective-permute-start.4 = (bf16[128,1024]{1,0:T(8,128)(2,1)S(1)}, bf16[128,1024]{1,0:T(8,128)(2,1)S(1)}, u32[]{:S(2)}, u32[]{:S(2)}) collective-permute-start(bf16[128,1024]{1,0:T(8,128)(2,1)S(1)} %fusion.60), channel_id=1, source_target_pairs={{1,0},{2,1},{3,2},{4,3},{5,4},{6,5},{7,6},{8,7},{9,8},{10,9},{11,1... | collective-permute-start | bytes 786440 | tf_op jit(solution)/shard_map/ppermute | solution.py:18
  46.7 14.3 %copy-start.9 = (bf16[128,1024]{1,0:T(8,128)(2,1)}, bf16[128,1024]{1,0:T(8,128)(2,1)S(1)}, u32[]{:S(2)}) copy-start(bf16[128,1024]{1,0:T(8,128)(2,1)S(1)} %collective-permute-done) | copy-start | bytes 786436
  46.7 5.9 %collective-permute-start.1 = (bf16[128,1024]{1,0:T(8,128)(2,1)S(1)}, bf16[128,1024]{1,0:T(8,128)(2,1)}, u32[]{:S(2)}, u32[]{:S(2)}) collective-permute-start(bf16[128,1024]{1,0:T(8,128)(2,1)S(1)} %collective-permute-done), channel_id=1, source_target_pairs={{0,1},{1,2},{2,3},{3,4},{4,5},{5,6},{6,7},{7,8},{8,9},{9,10},{10,1... | collective-permute-start | bytes 786440 | tf_op jit(solution)/shard_map/ppermute | solution.py:18
  51.3 9.7 %copy-start.7 = (bf16[128,1024]{1,0:T(8,128)(2,1)}, bf16[128,1024]{1,0:T(8,128)(2,1)S(1)}, u32[]{:S(2)}) copy-start(bf16[128,1024]{1,0:T(8,128)(2,1)S(1)} %collective-permute-done.4) | copy-start | bytes 786436
  51.3 8.4 %collective-permute-start.5 = (bf16[128,1024]{1,0:T(8,128)(2,1)S(1)}, bf16[128,1024]{1,0:T(8,128)(2,1)}, u32[]{:S(2)}, u32[]{:S(2)}) collective-permute-start(bf16[128,1024]{1,0:T(8,128)(2,1)S(1)} %collective-permute-done.4), channel_id=1, source_target_pairs={{1,0},{2,1},{3,2},{4,3},{5,4},{6,5},{7,6},{8,7},{9,8},{10,9},{11,1... | collective-permute-start | bytes 786440 | tf_op jit(solution)/shard_map/ppermute | solution.py:18
  52.6 8.4 %collective-permute-start.2 = (bf16[128,1024]{1,0:T(8,128)(2,1)}, bf16[128,1024]{1,0:T(8,128)(2,1)}, u32[]{:S(2)}, u32[]{:S(2)}) collective-permute-start(bf16[128,1024]{1,0:T(8,128)(2,1)} %collective-permute-done.1), channel_id=1, source_target_pairs={{0,1},{1,2},{2,3},{3,4},{4,5},{5,6},{6,7},{7,8},{8,9},{9,10},{10,1... | collective-permute-start | bytes 786440 | tf_op jit(solution)/shard_map/ppermute | solution.py:18
  59.7 12.4 %collective-permute-start.6 = (bf16[128,1024]{1,0:T(8,128)(2,1)}, bf16[128,1024]{1,0:T(8,128)(2,1)}, u32[]{:S(2)}, u32[]{:S(2)}) collective-permute-start(bf16[128,1024]{1,0:T(8,128)(2,1)} %collective-permute-done.5), channel_id=1, source_target_pairs={{1,0},{2,1},{3,2},{4,3},{5,4},{6,5},{7,6},{8,7},{9,8},{10,9},{11,1... | collective-permute-start | bytes 786440 | tf_op jit(solution)/shard_map/ppermute | solution.py:18
  61.0 12.4 %collective-permute-start.3 = (bf16[128,1024]{1,0:T(8,128)(2,1)}, bf16[128,1024]{1,0:T(8,128)(2,1)}, u32[]{:S(2)}, u32[]{:S(2)}) collective-permute-start(bf16[128,1024]{1,0:T(8,128)(2,1)} %collective-permute-done.2), channel_id=1, source_target_pairs={{0,1},{1,2},{2,3},{3,4},{4,5},{5,6},{6,7},{7,8},{8,9},{9,10},{10,1... | collective-permute-start | bytes 786440 | tf_op jit(solution)/shard_map/ppermute | solution.py:18
  72.1 15.8 %collective-permute-start.7 = (bf16[128,1024]{1,0:T(8,128)(2,1)}, bf16[128,1024]{1,0:T(8,128)(2,1)S(1)}, u32[]{:S(2)}, u32[]{:S(2)}) collective-permute-start(bf16[128,1024]{1,0:T(8,128)(2,1)} %collective-permute-done.6), channel_id=1, source_target_pairs={{1,0},{2,1},{3,2},{4,3},{5,4},{6,5},{7,6},{8,7},{9,8},{10,9},{11,1... | collective-permute-start | bytes 786440 | tf_op jit(solution)/shard_map/ppermute | solution.py:18
  73.4 9.4 %slice-start = ((s8[6291456]{0:T(1024)(128)(4,1)}), s8[4194304]{0:T(1024)(128)(4,1)S(1)}, s32[]{:S(2)}) async-start(s8[6291456]{0:T(1024)(128)(4,1)} %bitcast.101), calls=%async_computation.5 | async-start | bytes 8388608
  76.6 6.2 %slice-start.1 = ((s8[6291456]{0:T(1024)(128)(4,1)}), s8[2097152]{0:T(1024)(128)(4,1)S(1)}, s32[]{:S(2)}) async-start(s8[6291456]{0:T(1024)(128)(4,1)} %bitcast.101), calls=%async_computation.6 | async-start | bytes 4194304
  76.6 6.2 %copy-start.10 = (bf16[128,1024]{1,0:T(8,128)(2,1)S(1)}, bf16[128,1024]{1,0:T(8,128)(2,1)}, u32[]{:S(2)}) copy-start(bf16[128,1024]{1,0:T(8,128)(2,1)} %copy-done.9) | copy-start | bytes 786436
  82.8 1.0 copy-start.8
  88.6 2.1 copy-start.3
  95.5 8.4 %copy-start.4 = (bf16[128,1024]{0,1:T(8,128)(2,1)S(1)}, bf16[128,1024]{0,1:T(8,128)(2,1)}, u32[]{:S(2)}) copy-start(bf16[128,1024]{0,1:T(8,128)(2,1)} %copy.27) | copy-start | bytes 786436
  109.4 4.2 %copy-start.2 = (bf16[128,1024]{1,0:T(8,128)(2,1)S(1)}, bf16[128,1024]{1,0:T(8,128)(2,1)}, u32[]{:S(2)}) copy-start(bf16[128,1024]{1,0:T(8,128)(2,1)} %param.15) | copy-start | bytes 786436
  126.3 4.7 %copy-start.5 = (bf16[128,1024]{0,1:T(8,128)(2,1)S(1)}, bf16[128,1024]{0,1:T(8,128)(2,1)}, u32[]{:S(2)}) copy-start(bf16[128,1024]{0,1:T(8,128)(2,1)} %copy.27) | copy-start | bytes 786436
  190.9 2.1 copy-start.1
  194.6 22.1 %collective-permute-start.8 = (bf16[128,2048]{1,0:T(8,128)(2,1)S(1)}, bf16[128,2048]{1,0:T(8,128)(2,1)}, u32[]{:S(2)}, u32[]{:S(2)}) collective-permute-start(bf16[128,2048]{1,0:T(8,128)(2,1)S(1)} %get-tuple-element.8), channel_id=1, source_target_pairs={{0,1},{1,2},{2,3},{3,4},{4,5},{5,6},{6,7},{7,8},{8,9},{9,10},{10,1... | collective-permute-start | bytes 1572872 | tf_op jit(solution)/shard_map/ppermute | solution.py:18
  200.0 18.7 %collective-permute-start.15 = (bf16[128,2048]{1,0:T(8,128)(2,1)S(1)}, bf16[128,2048]{1,0:T(8,128)(2,1)}, u32[]{:S(2)}, u32[]{:S(2)}) collective-permute-start(bf16[128,2048]{1,0:T(8,128)(2,1)S(1)} %get-tuple-element.9), channel_id=1, source_target_pairs={{4,0},{5,1},{6,2},{7,3},{8,4},{9,5},{10,6},{11,7},{12,8},{13,9},{1... | collective-permute-start | bytes 1572872 | tf_op jit(solution)/shard_map/ppermute | solution.py:18
  201.3 22.0 %collective-permute-start.14 = (bf16[128,2048]{1,0:T(8,128)(2,1)S(1)}, bf16[128,2048]{1,0:T(8,128)(2,1)}, u32[]{:S(2)}, u32[]{:S(2)}) collective-permute-start(bf16[128,2048]{1,0:T(8,128)(2,1)S(1)} %get-tuple-element.10), channel_id=1, source_target_pairs={{0,4},{1,5},{2,6},{3,7},{4,8},{5,9},{6,10},{7,11},{8,12},{9,13},{1... | collective-permute-start | bytes 1572872 | tf_op jit(solution)/shard_map/ppermute | solution.py:18
  208.6 35.4 %collective-permute-start.13 = (bf16[128,2048]{1,0:T(8,128)(2,1)}, bf16[128,2048]{1,0:T(8,128)(2,1)}, u32[]{:S(2)}, u32[]{:S(2)}) collective-permute-start(bf16[128,2048]{1,0:T(8,128)(2,1)} %get-tuple-element.11), channel_id=1, source_target_pairs={{3,0},{4,1},{5,2},{6,3},{7,4},{8,5},{9,6},{10,7},{11,8},{12,9},{13... | collective-permute-start | bytes 1572872 | tf_op jit(solution)/shard_map/ppermute | solution.py:18
  210.1 35.6 %collective-permute-start.12 = (bf16[128,2048]{1,0:T(8,128)(2,1)}, bf16[128,2048]{1,0:T(8,128)(2,1)}, u32[]{:S(2)}, u32[]{:S(2)}) collective-permute-start(bf16[128,2048]{1,0:T(8,128)(2,1)} %get-tuple-element.12), channel_id=1, source_target_pairs={{0,3},{1,4},{2,5},{3,6},{4,7},{5,8},{6,9},{7,10},{8,11},{9,12},{10... | collective-permute-start | bytes 1572872 | tf_op jit(solution)/shard_map/ppermute | solution.py:18
  216.7 29.0 %collective-permute-start.11 = (bf16[128,2048]{1,0:T(8,128)(2,1)}, bf16[128,2048]{1,0:T(8,128)(2,1)}, u32[]{:S(2)}, u32[]{:S(2)}) collective-permute-start(bf16[128,2048]{1,0:T(8,128)(2,1)} %get-tuple-element.13), channel_id=1, source_target_pairs={{2,0},{3,1},{4,2},{5,3},{6,4},{7,5},{8,6},{9,7},{10,8},{11,9},{12,... | collective-permute-start | bytes 1572872 | tf_op jit(solution)/shard_map/ppermute | solution.py:18
  218.7 36.2 %collective-permute-start.10 = (bf16[128,2048]{1,0:T(8,128)(2,1)}, bf16[128,2048]{1,0:T(8,128)(2,1)}, u32[]{:S(2)}, u32[]{:S(2)}) collective-permute-start(bf16[128,2048]{1,0:T(8,128)(2,1)} %get-tuple-element.14), channel_id=1, source_target_pairs={{0,2},{1,3},{2,4},{3,5},{4,6},{5,7},{6,8},{7,9},{8,10},{9,11},{10,... | collective-permute-start | bytes 1572872 | tf_op jit(solution)/shard_map/ppermute | solution.py:18
  223.3 31.5 %collective-permute-start.9 = (bf16[128,2048]{1,0:T(8,128)(2,1)}, bf16[128,2048]{1,0:T(8,128)(2,1)}, u32[]{:S(2)}, u32[]{:S(2)}) collective-permute-start(bf16[128,2048]{1,0:T(8,128)(2,1)} %get-tuple-element.15), channel_id=1, source_target_pairs={{1,0},{2,1},{3,2},{4,3},{5,4},{6,5},{7,6},{8,7},{9,8},{10,9},{11,1... | collective-permute-start | bytes 1572872 | tf_op jit(solution)/shard_map/ppermute | solution.py:18
  243.8 14.2 %copy-start.6 = (f32[1024]{0:T(1024)S(1)}, f32[1024]{0:T(1024)}, u32[]{:S(2)}) copy-start(f32[1024]{0:T(1024)} %param.12) | copy-start | bytes 12292
  264.9 40.8 %all-to-all-start.2 = ((bf16[16,8,1024]{2,1,0:T(8,128)(2,1)}), bf16[16,8,1024]{2,1,0:T(8,128)(2,1)S(1)}, u32[]{:S(2)}, u32[]{:S(2)}) async-start(bf16[16,8,1024]{2,1,0:T(8,128)(2,1)} %bitcast.33), calls=%async_computation.2 | async-start | bytes 524288 | tf_op jit(solution)/shard_map/all_to_all | solution.py:132
Sparse Core Ops, SparseCore 0:
  116.4 77.8 reduce-scatter.1
where the time goes:
time: 318 us; the launch traced here: 316 us
  matrix products  85.7 us (27%)
  blocking collectives  60.1 us (19%)
  starting transfers between devices  58.8 us (18%)
  local copies, waits for them, and re-layouts  50.4 us (16%)
  other arithmetic  34.2 us (11%)
  between operations  15.2 us (5%)
  waiting for transfers between devices  11.7 us (4%)
    ppermute x16, starting transfers between devices, from_behind(): return lax.ppermute(block, axis, route)  53.5 us
    psum x1, blocking collectives, per_device(): grad_gain = lax.psum(gain_term, 'ctx') * norm_scale  33.8 us
    dot_general x1, matrix products, per_device(): jnp.einsum('shqk,sqhd->skhd', d_scores, heads_q, preferred_element_type=j...  19.2 us
    dot_general x1, matrix products, per_device(): jnp.einsum('shqk,skhd->sqhd', d_scores, heads_k, preferred_element_type=j...  19.1 us
    dot_general x8, matrix products, per_device(): jnp.dot(remote_piece, kv_weight, preferred_element_type=jnp.float32)  14.8 us
    all_to_all x1, blocking collectives, per_device(): lax.all_to_all(wanted, 'ctx', split_axis=0, concat_axis=0, tiled=True)  13.6 us
    all_to_all x1, blocking collectives, per_device(): lax.all_to_all(outgoing, 'ctx', split_axis=0, concat_axis=0, tiled=True)  12.6 us
    scatter-add x1, other arithmetic, per_device(): jnp.zeros(window_blocks.shape, jnp.float32).at[slot_index.reshape(-1)]  12.3 us
  transfers between devices with their start and end apart: 18, of which 3 were waited for; matrix products, arithmetic and copies ran while one was open for 40% of the time, Pallas kernels for 0%

commit v1 on v0

v1 whole, which is shorter than its diff:
```python
import functools

import jax
import jax.numpy as jnp
from jax import lax
from jax.experimental import pallas as pl
from jax.experimental.pallas import tpu as pltpu
from jax.sharding import PartitionSpec as P

HEADS = 16
BLOCK = 128
REACH = 4
MOST = 5
EPS = 1e-06
FAR = -1e30
PLANE = 4
ROWS = 16
TILE = 256
F32 = jnp.float32
BF16 = jnp.bfloat16
MESH = pl.DeviceIdType.MESH


def dot(a, b):
    return jnp.dot(a, b, preferred_element_type=F32)


def dot_t(a, b):
    return lax.dot_general(a, b, (((1,), (1,)), ((), ())), preferred_element_type=F32)


def kernel(
    n,
    perm_ref, nb_ref, cnt_ref, raster_ref, gain_ref, wqkv_hbm, wout_hbm, cot_ref,
    layer_ref, gtok_ref, gwout_ref, ggain_ref,
    wqkv, wout, e_ref, s_ref, req_out, req_in, tok_out, tok_in, ret_out, ret_in,
    gain_all, ordered, q_ref, da_ref, att_ref, dq_ref, win, sel, kv, dkvt, contrib, self_t,
    pair_out, pair_in, sum_out, sum_in, at_out, at_all, cot_all, gw_out, gw_in, dord,
    a2a, wsend, wrecv, psend, precv, bsend, brecv, psem, gsend, grecv, wsem,
):
    tok, width = raster_ref.shape
    per_peer = tok // n
    folds = ROWS // per_peer
    chunk = width // folds
    rows = n * ROWS
    hd = width // HEADS
    scale = hd ** (-0.5)
    norm_scale = (tok * n) ** (-0.5)
    planes = n // PLANE
    own_rows = width // n
    me = lax.axis_index("ctx")
    partner = me + 1 - 2 * lax.rem(me, 2)
    odd = lax.rem(me, 2)
    plane = me // PLANE
    spot = lax.rem(me, PLANE)

    def remote(src, dst, ssem, rsem, dev):
        return pltpu.make_async_remote_copy(
            src_ref=src, dst_ref=dst, send_sem=ssem, recv_sem=rsem,
            device_id={"ctx": dev}, device_id_type=MESH,
        )

    w1 = pltpu.make_async_copy(wqkv_hbm, wqkv, wsem.at[0])
    w2 = pltpu.make_async_copy(wout_hbm, wout, wsem.at[1])
    w1.start()
    w2.start()
    barrier = pltpu.get_barrier_semaphore()

    @pl.loop(1, n)
    def _(k):
        pl.semaphore_signal(
            barrier, inc=1, device_id={"ctx": lax.rem(me + k, n)}, device_id_type=MESH
        )

    shift = tok.bit_length() - 1
    perm = perm_ref[...]
    src = perm >> shift
    local = (perm & (tok - 1)).astype(F32)
    ii = lax.broadcasted_iota(jnp.int32, (tok, tok), 0)
    jj = lax.broadcasted_iota(jnp.int32, (tok, tok), 1)
    src_f = jnp.broadcast_to(src.astype(F32), (tok, tok))
    src_col = jnp.sum(jnp.where(ii == jj, src_f, 0.0), axis=1, keepdims=True)
    rank = jnp.sum(jnp.where((src_col == src_f) & (ii < jj), 1.0, 0.0), axis=0, keepdims=True)
    rank = rank.astype(jnp.int32)
    kk = lax.broadcasted_iota(jnp.int32, (rows, tok), 0)
    hit = ((kk >> (ROWS.bit_length() - 1)) == src) & ((kk & (per_peer - 1)) == rank)
    e_ref[...] = jnp.where(hit, 1.0, 0.0)
    want = jnp.sum(jnp.where(hit, local, 0.0), axis=1, keepdims=True).astype(jnp.int32)
    req_out[...] = jnp.broadcast_to(want, (rows, tok)).reshape(n, ROWS, tok)
    req_in[me] = req_out[me]

    pl.semaphore_wait(barrier, n - 1)

    def a2a_copy(kind, k, src, dst, landed, mine):
        peer = lax.rem(me + k, n)
        source = lax.rem(me + n - k, n)
        return remote(
            src.at[me if mine else peer], dst.at[source if landed else me],
            a2a.at[kind, 0, k], a2a.at[kind, 1, k], peer,
        )

    def a2a_start(kind, src, dst, mine=False):
        @pl.loop(1, n)
        def _(k):
            a2a_copy(kind, k, src, dst, False, mine).start()

    def a2a_recv(kind, src, dst, mine=False):
        @pl.loop(1, n)
        def _(k):
            a2a_copy(kind, k, src, dst, True, mine).wait_recv()

    def a2a_sent(kind, src, dst, mine=False):
        @pl.loop(1, n)
        def _(k):
            a2a_copy(kind, k, src, dst, True, mine).wait_send()

    fold_shift = per_peer.bit_length() - 1

    def pack(onehot, x_ref, out):
        total = None
        fold = (kk >> fold_shift) & (folds - 1)
        for f in range(folds):
            part = dot(
                jnp.where(fold == f, onehot, 0.0).astype(BF16),
                x_ref[:, f * chunk : (f + 1) * chunk],
            )
            total = part if total is None else total + part
        out[...] = total.astype(BF16).reshape(n, ROWS, chunk)

    def unpack(onehot, y_ref, out):
        turned = onehot.T
        kt = lax.broadcasted_iota(jnp.int32, (tok, rows), 1)
        fold = (kt >> fold_shift) & (folds - 1)
        y = y_ref[...].reshape(rows, chunk)
        for f in range(folds):
            out[:, f * chunk : (f + 1) * chunk] = dot(
                jnp.where(fold == f, turned, 0.0).astype(BF16), y
            ).astype(BF16)

    a2a_start(0, req_out, req_in)
    a2a_recv(0, req_out, req_in)
    s_ref[...] = jnp.where(
        req_in[...].reshape(rows, tok) == lax.broadcasted_iota(jnp.int32, (rows, tok), 1), 1.0, 0.0
    )
    pack(s_ref[...], raster_ref, tok_out)
    a2a_start(1, tok_out, tok_in)
    tok_in[me] = tok_out[me]
    a2a_sent(0, req_out, req_in)
    a2a_recv(1, tok_out, tok_in)
    unpack(e_ref[...], tok_in, ordered)
    ord_f = ordered[...].astype(F32)
    inv_rms = lax.rsqrt(jnp.mean(ord_f * ord_f, axis=-1, keepdims=True) + EPS)
    gain = gain_ref[...]
    win[REACH] = (ord_f * inv_rms * gain).astype(BF16)

    def inside(b):
        return (b >= 0) & (b < n)

    hops = (-2, 2, -4, 4)

    def win_copy(t):
        return remote(win.at[REACH], win.at[REACH - t], wsend.at[REACH - t], wrecv.at[REACH - t], me + t)

    delta = me - partner

    def pass_copy(e):
        slot = REACH + e + delta
        return remote(win.at[REACH + e], win.at[slot], wsend.at[slot], wrecv.at[slot], partner)

    for t in hops:
        @pl.when(inside(me + t))
        def _():
            win_copy(t).start()
    pass_copy(0).start()

    w1.wait()
    w2.wait()

    @pl.loop(0, width // TILE)
    def _(t):
        cols = pl.ds(pl.multiple_of(t * TILE, TILE), TILE)
        q_ref[:, cols] = (dot(win[REACH], wqkv[:, cols]).astype(BF16).astype(F32) * scale).astype(BF16)
        da_ref[:, cols] = dot_t(cot_ref[...], wout[cols, :]).astype(BF16)

    def passes(e):
        near = inside(me + e)
        if e == -4:
            return near & (odd == 1)
        if e == 4:
            return near & (odd == 0)
        return near

    def arrive(e):
        slot = REACH + e
        return remote(win.at[REACH], win.at[slot], wsend.at[slot], wrecv.at[slot], partner)

    for e in hops:
        @pl.when(inside(me + e))
        def _():
            arrive(e).wait_recv()

        @pl.when(passes(e))
        def _():
            pass_copy(e).start()

    for e in (-1, 1, -3, 3):
        @pl.when(inside(me + e))
        def _():
            arrive(e).wait_recv()

    base = plane * PLANE

    def mate(k):
        return base + lax.rem(spot + k, PLANE)

    def cot_copy(k, where):
        return remote(cot_ref, cot_all.at[where], psem.at[0, 0, k], psem.at[0, 1, k], mate(k))

    for k in range(1, PLANE):
        cot_copy(k, spot).start()
    cot_all[spot] = cot_ref[...]

    for j in range(MOST):
        sel[j * BLOCK : (j + 1) * BLOCK, :] = win[
            jnp.clip(nb_ref[0, j] - me + REACH, 0, 2 * REACH)
        ]

    @pl.loop(0, 2 * width // TILE)
    def _(t):
        cols = pl.ds(pl.multiple_of(t * TILE, TILE), TILE)
        wcols = pl.ds(pl.multiple_of(width + t * TILE, TILE), TILE)
        kv[:, cols] = dot(sel[...], wqkv[:, wcols]).astype(BF16)

    count = cnt_ref[0]
    keys = MOST * BLOCK
    slot_of = lax.broadcasted_iota(jnp.int32, (1, keys), 1) >> (BLOCK.bit_length() - 1)
    bias = jnp.where(slot_of < count, 0.0, FAR)
    pair = 2 * hd
    low = lax.broadcasted_iota(jnp.int32, (tok, pair), 1) < hd
    blocks_per_pair = pair // own_rows

    def stacked(x):
        x = x.astype(F32)
        return jnp.concatenate([jnp.where(low, x, 0.0), jnp.where(low, 0.0, x)], axis=0)

    @pl.loop(0, HEADS // 2)
    def _(h):
        cols = pl.ds(pl.multiple_of(h * pair, pair), pair)
        vcols = pl.ds(pl.multiple_of(width + h * pair, pair), pair)
        qs = stacked(q_ref[:, cols])
        ds = stacked(da_ref[:, cols])
        k = kv[:, cols]
        v = kv[:, vcols]
        scores = dot_t(qs.astype(BF16), k) + bias
        top = jnp.max(scores, axis=-1, keepdims=True)
        raised = jnp.exp(scores - top)
        probs = raised * (1.0 / jnp.sum(raised, axis=-1, keepdims=True))
        probs_b = probs.astype(BF16)
        out = dot(probs_b, v)
        att = jnp.where(low, out[:tok], out[tok:])
        att_ref[:, cols] = att.astype(BF16)
        att_t = att.T.astype(BF16)
        for b in range(blocks_per_pair):
            block = h * blocks_per_pair + b
            at_out[lax.rem(block, PLANE) * planes + block // PLANE] = att_t[
                b * own_rows : (b + 1) * own_rows
            ]
        d_probs = dot_t(ds.astype(BF16), v)
        dots = jnp.sum(d_probs * probs, axis=-1, keepdims=True)
        d_scores = (probs * (d_probs - dots)).astype(BF16)
        dq = dot(d_scores, k) * scale
        dq_ref[:, cols] = jnp.where(low, dq[:tok], dq[tok:]).astype(BF16)
        dkvt[cols, :] = dot(qs.T.astype(BF16), d_scores).astype(BF16)
        dkvt[vcols, :] = dot(ds.T.astype(BF16), probs_b).astype(BF16)

    def at_copy(k, where):
        return remote(
            at_out.at[pl.ds(lax.rem(spot + k, PLANE) * planes, planes)], at_all.at[where],
            psem.at[1, 0, k], psem.at[1, 1, k], mate(k),
        )

    for k in range(1, PLANE):
        at_copy(k, spot).start()
    at_all[spot] = at_out[pl.ds(spot * planes, planes)]

    contrib[MOST] = jnp.zeros((width, BLOCK), BF16)

    @pl.loop(0, width // TILE)
    def _(t):
        at = pl.ds(pl.multiple_of(t * TILE, TILE), TILE)
        part = dot(wqkv[at, width:], dkvt[...])
        self_t[at, :] = part[:, :BLOCK]
        part = part.astype(BF16)
        for j in range(MOST):
            contrib[j, at, :] = part[:, j * BLOCK : (j + 1) * BLOCK]

    def holder(w):
        found = jnp.int32(MOST)
        for j in range(1, MOST):
            found = jnp.where((nb_ref[0, j] - me + REACH == w) & (j < count), j, found)
        return found

    def pair_copy(m):
        return remote(pair_out.at[m], pair_in.at[m], psend.at[m], precv.at[m], partner)

    for m, d in enumerate((-3, -1, 1, 3)):
        pair_out[m] = contrib[holder(REACH + d)]
        pair_copy(m).start()

    def from_pair(e):
        m = e // 2 + 1 + odd
        got = pair_in[jnp.clip(m, 0, 3)].astype(F32)
        if e == -4:
            return jnp.where(odd == 1, got, 0.0)
        if e == 4:
            return jnp.where(odd == 0, got, 0.0)
        return got

    def sum_copy(t):
        return remote(
            sum_out.at[REACH + t], sum_in.at[REACH - t], bsend.at[REACH - t], brecv.at[REACH - t], me + t
        )

    for m in range(4):
        pair_copy(m).wait_recv()
    for t in hops:
        @pl.when(inside(me + t))
        def _():
            both = contrib[holder(REACH + t)].astype(F32) + from_pair(t)
            sum_out[REACH + t] = both.astype(BF16)
            sum_copy(t).start()

    for k in range(1, PLANE):
        here = lax.rem(spot + PLANE - k, PLANE)
        cot_copy(k, here).wait_recv()
        at_copy(k, here).wait_recv()
    lhs = jnp.concatenate([at_all[i].reshape(width // PLANE, tok) for i in range(PLANE)], axis=1)

    @pl.loop(0, width // TILE)
    def _(t):
        cols = pl.ds(pl.multiple_of(t * TILE, TILE), TILE)
        part = dot(lhs, cot_all[:, :, cols].reshape(PLANE * tok, TILE)).reshape(planes, own_rows, TILE)
        gw_out[:, :, cols] = part.astype(BF16)

    def gw_copy(k, where):
        to = lax.rem(plane + k, planes)
        return remote(
            gw_out.at[to], gw_in.at[where], gsend.at[k], grecv.at[k], to * PLANE + spot
        )

    @pl.loop(1, planes)
    def _(k):
        gw_copy(k, plane).start()

    gw_in[plane] = gw_out[plane]

    @pl.loop(0, width // TILE)
    def _(t):
        cols = pl.ds(pl.multiple_of(t * TILE, TILE), TILE)
        layer_ref[:, cols] = (
            ordered[:, cols].astype(F32) + dot(att_ref[...], wout[:, cols])
        ).astype(BF16)

    self_t[...] += from_pair(0)
    for t in hops:
        @pl.when(inside(me + t))
        def _():
            slot = REACH + t
            remote(
                sum_out.at[slot], sum_in.at[slot], bsend.at[slot], brecv.at[slot], partner
            ).wait_recv()
            self_t[...] += sum_in[slot].astype(F32)

    d_normed = self_t[...].T + dot_t(dq_ref[...], wqkv[:, :width])
    gain_all[me] = jnp.sum(d_normed * ord_f * inv_rms, axis=0, keepdims=True)
    a2a_start(3, gain_all, gain_all, True)
    scaled = d_normed * gain
    dord[...] = (
        cot_ref[...].astype(F32)
        + inv_rms * scaled
        - ord_f * (inv_rms * inv_rms * inv_rms) * jnp.mean(scaled * ord_f, axis=-1, keepdims=True)
    ).astype(BF16)
    pack(e_ref[...], dord, ret_out)
    a2a_start(2, ret_out, ret_in)
    ret_in[me] = ret_out[me]

    @pl.loop(1, planes)
    def _(k):
        gw_copy(k, lax.rem(plane + planes - k, planes)).wait_recv()

    total = gw_in[0].astype(F32)
    for z in range(1, planes):
        total = total + gw_in[z].astype(F32)
    gwout_ref[...] = total * norm_scale

    a2a_recv(3, gain_all, gain_all, True)
    ggain_ref[...] = jnp.sum(gain_all[...], axis=0) * norm_scale
    a2a_recv(2, ret_out, ret_in)
    unpack(s_ref[...], ret_in, gtok_ref)

    a2a_sent(1, tok_out, tok_in)
    a2a_sent(2, ret_out, ret_in)
    a2a_sent(3, gain_all, gain_all, True)
    for t in hops:
        @pl.when(inside(me + t))
        def _():
            win_copy(t).wait_send()
            sum_copy(t).wait_send()

        @pl.when(passes(t))
        def _():
            pass_copy(t).wait_send()
    pass_copy(0).wait_send()
    for m in range(4):
        pair_copy(m).wait_send()
    for k in range(1, PLANE):
        cot_copy(k, spot).wait_send()
        at_copy(k, spot).wait_send()

    @pl.loop(1, planes)
    def _(k):
        gw_copy(k, plane).wait_send()


def per_device(
    raster_tokens, hilbert_perm, neighbors, neighbor_counts, norm_gain, w_qkv, w_out, cotangent
):
    n = lax.axis_size("ctx")
    tok, width = raster_tokens.shape
    per_peer = tok // n
    assert tok == BLOCK and n % PLANE == 0 and ROWS % per_peer == 0
    chunk = width * per_peer // ROWS
    planes = n // PLANE
    own_rows = width // n
    rows = n * ROWS
    vmem = pl.BlockSpec(memory_space=pltpu.VMEM)
    smem = pl.BlockSpec(memory_space=pltpu.SMEM)
    hbm = pl.BlockSpec(memory_space=pl.ANY)
    V = pltpu.VMEM
    dma = pltpu.SemaphoreType.DMA
    span = 2 * REACH + 1
    scratch = [
        V((width, 3 * width), BF16),
        V((width, width), BF16),
        V((rows, tok), F32),
        V((rows, tok), F32),
        V((n, ROWS, tok), jnp.int32),
        V((n, ROWS, tok), jnp.int32),
        V((n, ROWS, chunk), BF16),
        V((n, ROWS, chunk), BF16),
        V((n, ROWS, chunk), BF16),
        V((n, ROWS, chunk), BF16),
        V((n, 1, width), F32),
        V((tok, width), BF16),
        V((tok, width), BF16),
        V((tok, width), BF16),
        V((tok, width), BF16),
        V((tok, width), BF16),
        V((span, tok, width), BF16),
        V((MOST * BLOCK, width), BF16),
        V((MOST * BLOCK, 2 * width), BF16),
        V((2 * width, MOST * BLOCK), BF16),
        V((MOST + 1, width, BLOCK), BF16),
        V((width, tok), F32),
        V((4, width, BLOCK), BF16),
        V((4, width, BLOCK), BF16),
        V((span, width, BLOCK), BF16),
        V((span, width, BLOCK), BF16),
        V((n, own_rows, tok), BF16),
        V((PLANE, planes, own_rows, tok), BF16),
        V((PLANE, tok, width), BF16),
        V((planes, own_rows, width), BF16),
        V((planes, own_rows, width), BF16),
        V((tok, width), BF16),
        dma((4, 2, n)),
        dma((span,)),
        dma((span,)),
        dma((4,)),
        dma((4,)),
        dma((span,)),
        dma((span,)),
        dma((2, 2, PLANE)),
        dma((planes,)),
        dma((planes,)),
        dma((2,)),
    ]
    layer_out, grad_tokens, grad_w_out, grad_gain = pl.pallas_call(
        functools.partial(kernel, n),
        out_shape=(
            jax.ShapeDtypeStruct((tok, width), BF16),
            jax.ShapeDtypeStruct((tok, width), BF16),
            jax.ShapeDtypeStruct((own_rows, width), F32),
            jax.ShapeDtypeStruct((1, width), F32),
        ),
        in_specs=[vmem, smem, smem, vmem, vmem, hbm, hbm, vmem],
        out_specs=(vmem, vmem, vmem, vmem),
        scratch_shapes=scratch,
        compiler_params=pltpu.CompilerParams(
            collective_id=0, has_side_effects=True, vmem_limit_bytes=56 * 1024 * 1024
        ),
    )(
        hilbert_perm.reshape(1, tok), neighbors, neighbor_counts, raster_tokens,
        norm_gain.reshape(1, width), w_qkv, w_out, cotangent,
    )
    return (layer_out, grad_tokens, grad_w_out, grad_gain.reshape(width))


def solution(mesh):
    placed = (
        P(("groups", "ctx"), None),
        P(("groups", "ctx")),
        P(("groups", "ctx"), None),
        P(("groups", "ctx")),
        P(),
        P(),
        P(),
        P(("groups", "ctx"), None),
    )
    return jax.shard_map(
        per_device,
        mesh=mesh,
        in_specs=placed,
        out_specs=(
            P(("groups", "ctx"), None),
            P(("groups", "ctx"), None),
            P(("groups", "ctx"), None),
            P("groups"),
        ),
        check_vma=False,
    )
```

time: 318 us -> 95.8 us (0.30)
  Pallas kernels: 0 us -> 88 us
  matrix products: 85.7 us -> 0 us
  blocking collectives: 60.1 us -> 0 us
  starting transfers between devices: 58.8 us -> 0 us
  local copies, waits for them, and re-layouts: 50.4 us -> 6.27 us
  other arithmetic: 34.2 us -> 0 us
  between operations: 15.2 us -> 1.29 us
  waiting for transfers between devices: 11.7 us -> 0 us
    pallas_call x0 -> x1, Pallas kernels: none -> 88 us  [per_device(): pl.pallas_call(functools.partial(kernel, n), out_shape=(jax.ShapeDtypeStr...]
    dot_general x18 -> x0, matrix products: 80.2 us -> none  [the longest x1 19.2 us: per_device(): jnp.einsum('shqk,sqhd->skhd', d_scores, heads_q, preferred_element_type=j...]
    ppermute x16 -> x0, starting transfers between devices: 53.5 us -> none  [from_behind(): return lax.ppermute(block, axis, route)]
    psum x1 -> x0, blocking collectives: 33.8 us -> none  [per_device(): grad_gain = lax.psum(gain_term, 'ctx') * norm_scale]
    all_to_all x2 -> x0, blocking collectives: 26.2 us -> none  [the longest x1 13.6 us: per_device(): lax.all_to_all(wanted, 'ctx', split_axis=0, concat_axis=0, tiled=True)]
    scatter-add x1 -> x0, other arithmetic: 12.3 us -> none  [per_device(): jnp.zeros(window_blocks.shape, jnp.float32).at[slot_index.reshape(-1)]]
    ppermute x16 -> x0, waiting for transfers between devices: 11.7 us -> none  [from_behind(): return lax.ppermute(block, axis, route)]
    gather x4 -> x0, local copies, waits for them, and re-layouts: 9.54 us -> none  [the longest x1 4.72 us: per_device(): gathered = window_blocks[slot_index].reshape(per_dev, -1, 2 * model_width)]
  transfers between devices with their start and end apart: 18 -> 0, of which waited for: 3 -> 0; matrix products, arithmetic and copies ran while one was open for 40% -> 0% of each run, Pallas kernels for 0% -> 0%
where the time goes in v1:
time: 95.8 us; the launch traced here: 95.5 us
  Pallas kernels  88 us (92%)
  local copies, waits for them, and re-layouts  6.27 us (7%)
  between operations  1.29 us (1%)
    pallas_call x1, Pallas kernels, per_device(): pl.pallas_call(functools.partial(kernel, n), out_shape=(jax.ShapeDtypeStr...  88 us
    unnamed x4, local copies, waits for them, and re-layouts  6.27 us

profile of v1, /device:TPU:0, one launch (start us, length us, event | category | flops | bytes accessed | tf_op | source)
XLA Modules:
  0.0 95.5 jit_solution(5793857558691375363)
XLA Ops:
  1.3 88.0 %shard_map.111 = (bf16[128,1024]{1,0:T(8,128)(2,1)}, bf16[128,1024]{1,0:T(8,128)(2,1)}, f32[64,1024]{1,0:T(8,128)}, f32[1,1024]{1,0:T(1,128)}) custom-call(s32[1,128]{1,0:T(1,128)} %bitcast.5, s32[1,5]{1,0:T(1,128)} %nb_ref.1, s32[1]{0:T(128)S(6)} %copy.16.cnt_ref, bf16[128,1024]{1,0:T(8,128)(2,1)} %raster_ref.1, f32[1,1024]{1,0:T(1,128)} %bitcast.3, ...), custom_call_target="tpu_custom_call" | custom-call | tf_op jit(solution)/shard_map/pallas_call | solution.py:487
  89.3 1.7 %copy.17 = bf16[128,1024]{1,0:T(8,128)(2,1)} copy(bf16[128,1024]{1,0:T(8,128)(2,1)} %get-tuple-element.16) | data formatting | bytes 524288
  90.9 1.7 %copy.18 = bf16[128,1024]{1,0:T(8,128)(2,1)} copy(bf16[128,1024]{1,0:T(8,128)(2,1)} %get-tuple-element.17) | data formatting | bytes 524288
  92.6 1.7 %copy.19 = f32[64,1024]{1,0:T(8,128)} copy(f32[64,1024]{1,0:T(8,128)} %get-tuple-element.18) | data formatting | bytes 524288
  94.3 1.3 %copy.20 = f32[1024]{0:T(1024)} copy(f32[1024]{0:T(1024)} %bitcast.4) | data formatting | bytes 8192
